TPU v7x, 256 devices: a whole 4x4x8 slice. The times are simulated.
256 devices in a mesh: row: 64 (over y, z, core), col: 4 (over x).
Axes of the slice: x: 4, y: 4, z: 8, core: 2. Of those that a mesh axis runs over, the one named last changes fastest.
Arguments:
- factor: float32 [16384, 64, 256], P('row', 'col'), may hold values from -0.046875 to 0.046875
- diag_inverse: float32 [16384, 2048], P('row'), as said below
- phenotypes: float32 [16384, 512], P('row', 'col'), may hold values from -6 to 6
Outputs:
- solution: float32 [16384, 512], P('row', 'col')
Inputs may be any that keep to these rules, and one draw needn't show every extreme that they name: `diag_inverse`: each 2048 x 2048 panel inverse is lower triangular with a diagonal between 0.5 and 1.5.
All inputs are finite; a program needn't handle non-finite values.
Results may differ from a plain program's by a relative error of at most 0.0001.
Values sent between devices are 32-bit elements; how exact they have to be, the bound alone decides.
No kernel may reach another device: no remote copies, remote signals or barrier semaphores. Data moves between devices by JAX's collectives and lax.ppermute only.
A program may use at most 128 MiB of HBM per device.

v0:
```python
import jax
import jax.numpy as jnp
from jax import lax
from jax.sharding import PartitionSpec as P


def shards(factor, diag_inverse, phenotypes):
    my_row = lax.axis_index("row")
    rows_here = phenotypes.shape[0]
    panel_rows = diag_inverse.shape[1]
    per_panel = panel_rows // rows_here
    my_panel = my_row // per_panel
    my_offset = my_row % per_panel * rows_here
    local_blocks = factor.shape[1]
    panel_count = local_blocks * lax.axis_size("col") // per_panel
    whole_factor = lax.all_gather(factor, "col", axis=1, tiled=True)
    flat_factor = whole_factor.reshape(rows_here, -1)
    empty = jnp.zeros(phenotypes.shape, jnp.float32)

    def solve_mine(residual):
        return lax.dot_general(
            diag_inverse,
            residual,
            (((0,), (0,)), ((), ())),
            precision=lax.Precision.HIGHEST,
            preferred_element_type=jnp.float32,
        )

    def solve_none(residual):
        return jnp.zeros((panel_rows, residual.shape[1]), jnp.float32)

    def advance(panel_index, carry):
        running, solved = carry
        columns = lax.dynamic_slice_in_dim(flat_factor, panel_index * panel_rows, panel_rows, 1)
        residual = phenotypes - running
        term = lax.cond(my_panel == panel_index, solve_mine, solve_none, residual)
        panel_solved = lax.psum(term, "row")
        mine = lax.dynamic_slice_in_dim(panel_solved, my_offset, rows_here, 0)
        solved = jnp.where(my_panel == panel_index, mine, solved)
        running = running + jnp.dot(
            columns,
            panel_solved,
            precision=lax.Precision.HIGHEST,
            preferred_element_type=jnp.float32,
        )
        return (running, solved)

    running, solution = lax.fori_loop(0, panel_count, advance, (empty, empty))
    return solution


def solution(mesh):
    placed = (P("row", "col", None), P("row", None), P("row", "col"))
    return jax.shard_map(
        shards, mesh=mesh, in_specs=placed, out_specs=P("row", "col"), check_vma=False
    )
```

profile of v0, /device:TPU:2, one launch (start us, length us, event | category | flops | bytes accessed | tf_op | source)
XLA Modules:
  0.0 1734.9 jit_solution(15123583881384055721)
XLA Ops:
  6.5 0.7 all-gather.2.cloned.1.call-update
  7.3 161.4 %all-gather.2.cloned.1.call-done = f32[256,64,256]{2,1,0:T(8,128)} async-done(((f32[256,16,256]{2,1,0:T(8,128)}), f32[256,64,256]{2,1,0:T(8,128)}) %all-gather.2.cloned.1.call-update) | async-done | bytes 16777232 | tf_op jit(solution)/shard_map/all_gather | solution.py:16
  168.7 18.6 %copy.5 = f32[32,8,64,256]{3,1,2,0:T(8,128)} copy(f32[32,8,64,256]{3,2,1,0:T(8,128)} %bitcast.9) | data formatting | bytes 33554432
  187.3 1540.3 %while.18 = (s32[]{:T(128)}, f32[256,128]{1,0:T(8,128)S(1)}, f32[256,128]{0,1:T(8,128)S(1)}, f32[256,16384]{1,0:T(8,128)}, s32[]{:T(128)}, /*index=5*/f32[256,12...) while((s32[]{:T(128)}, f32[256,128]{1,0:T(8,128)S(1)}, ...), condition=%wide.region_4.5_spmd.clone, body=%wide.region_0.4_spmd.clone.sunk | while | flops 1611038720 | bytes 17957160 | solution.py:48
  187.3 2.2 conditional.3
  187.4 2.1 convolution_bitcast_fusion
  189.5 1.0 copy-done
  190.6 187.4 %all-reduce.2.cloned.1.call-done = f32[2048,128]{0,1:T(8,128)} async-done(((f32[2048,128]{0,1:T(8,128)}), f32[2048,128]{0,1:T(8,128)}) %all-reduce.2.cloned.1.call-update) | async-done | bytes 1048592 | tf_op jit(solution)/shard_map/while/body/eval_jaxpr/psum | solution.py:37
  378.0 3.7 fusion.14
  381.7 0.9 select_select_fusion.2
  382.7 0.1 conditional.3
  382.8 1.0 copy-done
  383.9 186.4 %all-reduce.2.cloned.1.call-done = f32[2048,128]{0,1:T(8,128)} async-done(((f32[2048,128]{0,1:T(8,128)}), f32[2048,128]{0,1:T(8,128)}) %all-reduce.2.cloned.1.call-update) | async-done | bytes 1048592 | tf_op jit(solution)/shard_map/while/body/eval_jaxpr/psum | solution.py:37
  570.3 3.7 fusion.14
  574.0 0.9 select_select_fusion.2
  575.0 0.1 conditional.3
  575.1 0.1 broadcast.4
  575.2 1.0 copy-done
  576.2 186.1 %all-reduce.2.cloned.1.call-done = f32[2048,128]{0,1:T(8,128)} async-done(((f32[2048,128]{0,1:T(8,128)}), f32[2048,128]{0,1:T(8,128)}) %all-reduce.2.cloned.1.call-update) | async-done | bytes 1048592 | tf_op jit(solution)/shard_map/while/body/eval_jaxpr/psum | solution.py:37
  762.4 3.7 fusion.14
  766.0 0.9 select_select_fusion.2
  767.1 0.1 conditional.3
  767.1 0.1 broadcast.4
  767.2 1.0 copy-done
  768.3 185.6 %all-reduce.2.cloned.1.call-done = f32[2048,128]{0,1:T(8,128)} async-done(((f32[2048,128]{0,1:T(8,128)}), f32[2048,128]{0,1:T(8,128)}) %all-reduce.2.cloned.1.call-update) | async-done | bytes 1048592 | tf_op jit(solution)/shard_map/while/body/eval_jaxpr/psum | solution.py:37
  953.9 3.7 fusion.14
  957.5 0.9 select_select_fusion.2
  958.6 0.1 conditional.3
  958.7 1.0 copy-done
  959.7 186.1 %all-reduce.2.cloned.1.call-done = f32[2048,128]{0,1:T(8,128)} async-done(((f32[2048,128]{0,1:T(8,128)}), f32[2048,128]{0,1:T(8,128)}) %all-reduce.2.cloned.1.call-update) | async-done | bytes 1048592 | tf_op jit(solution)/shard_map/while/body/eval_jaxpr/psum | solution.py:37
  1145.9 3.7 fusion.14
  1149.6 0.9 select_select_fusion.2
  1150.6 0.1 conditional.3
  1150.7 1.0 copy-done
  1151.8 186.5 %all-reduce.2.cloned.1.call-done = f32[2048,128]{0,1:T(8,128)} async-done(((f32[2048,128]{0,1:T(8,128)}), f32[2048,128]{0,1:T(8,128)}) %all-reduce.2.cloned.1.call-update) | async-done | bytes 1048592 | tf_op jit(solution)/shard_map/while/body/eval_jaxpr/psum | solution.py:37
  1338.2 3.7 fusion.14
  1341.9 0.9 select_select_fusion.2
  1343.0 0.1 conditional.3
  1343.1 1.0 copy-done
  1344.1 186.5 %all-reduce.2.cloned.1.call-done = f32[2048,128]{0,1:T(8,128)} async-done(((f32[2048,128]{0,1:T(8,128)}), f32[2048,128]{0,1:T(8,128)}) %all-reduce.2.cloned.1.call-update) | async-done | bytes 1048592 | tf_op jit(solution)/shard_map/while/body/eval_jaxpr/psum | solution.py:37
  1530.6 3.7 fusion.14
  1534.3 0.9 select_select_fusion.2
  1535.3 0.1 conditional.3
  1535.5 1.0 copy-done
  1536.5 186.4 %all-reduce.2.cloned.1.call-done = f32[2048,128]{0,1:T(8,128)} async-done(((f32[2048,128]{0,1:T(8,128)}), f32[2048,128]{0,1:T(8,128)}) %all-reduce.2.cloned.1.call-update) | async-done | bytes 1048592 | tf_op jit(solution)/shard_map/while/body/eval_jaxpr/psum | solution.py:37
  1722.9 3.7 fusion.14
  1726.6 0.9 select_select_fusion.2
  1727.6 0.8 copy.4
  (42 shorter events, 1.0 us)
Async XLA Ops:
  6.5 162.2 %all-gather.2.cloned.1.call-start = ((), (), s32[]{:S(2)}) async-start(), calls=%async_computation | async-start | bytes 20971520 | tf_op jit(solution)/shard_map/all_gather | solution.py:16
  168.7 18.6 %copy-start.1 = (f32[256,2048]{1,0:T(8,128)S(1)}, f32[256,2048]{1,0:T(8,128)}, u32[]{:S(2)}) copy-start(f32[256,2048]{1,0:T(8,128)} %param.8) | copy-start | bytes 6291460
  187.3 190.7 %all-reduce.2.cloned.1.call-start = ((), (), s32[]{:S(2)}) async-start(), calls=%async_computation.1 | async-start | bytes 2097152 | tf_op jit(solution)/shard_map/while/body/eval_jaxpr/psum | solution.py:37
  189.5 1.0 copy-start
  382.6 187.7 %all-reduce.2.cloned.1.call-start = ((), (), s32[]{:S(2)}) async-start(), calls=%async_computation.1 | async-start | bytes 2097152 | tf_op jit(solution)/shard_map/while/body/eval_jaxpr/psum | solution.py:37
  382.8 1.0 copy-start
  575.0 187.4 %all-reduce.2.cloned.1.call-start = ((), (), s32[]{:S(2)}) async-start(), calls=%async_computation.1 | async-start | bytes 2097152 | tf_op jit(solution)/shard_map/while/body/eval_jaxpr/psum | solution.py:37
  575.2 1.0 copy-start
  767.0 186.8 %all-reduce.2.cloned.1.call-start = ((), (), s32[]{:S(2)}) async-start(), calls=%async_computation.1 | async-start | bytes 2097152 | tf_op jit(solution)/shard_map/while/body/eval_jaxpr/psum | solution.py:37
  767.2 1.0 copy-start
  958.5 187.4 %all-reduce.2.cloned.1.call-start = ((), (), s32[]{:S(2)}) async-start(), calls=%async_computation.1 | async-start | bytes 2097152 | tf_op jit(solution)/shard_map/while/body/eval_jaxpr/psum | solution.py:37
  958.7 1.0 copy-start
  1150.5 187.7 %all-reduce.2.cloned.1.call-start = ((), (), s32[]{:S(2)}) async-start(), calls=%async_computation.1 | async-start | bytes 2097152 | tf_op jit(solution)/shard_map/while/body/eval_jaxpr/psum | solution.py:37
  1150.7 1.0 copy-start
  1342.9 187.7 %all-reduce.2.cloned.1.call-start = ((), (), s32[]{:S(2)}) async-start(), calls=%async_computation.1 | async-start | bytes 2097152 | tf_op jit(solution)/shard_map/while/body/eval_jaxpr/psum | solution.py:37
  1343.1 1.0 copy-start
  1535.2 187.7 %all-reduce.2.cloned.1.call-start = ((), (), s32[]{:S(2)}) async-start(), calls=%async_computation.1 | async-start | bytes 2097152 | tf_op jit(solution)/shard_map/while/body/eval_jaxpr/psum | solution.py:37
  1535.4 1.0 copy-start
Sparse Core Ops, SparseCore 0:
  9.2 159.5 all-gather.1
  191.6 186.3 all-reduce.1
  386.9 183.4 all-reduce.1
  578.9 183.4 all-reduce.1
  771.0 182.8 all-reduce.1
  962.4 183.4 all-reduce.1
  1154.8 183.3 all-reduce.1
  1347.2 183.4 all-reduce.1
  1539.5 183.4 all-reduce.1
where the time goes:
time: 1740 us; the launch traced here: 1730 us
  waiting for transfers between devices  1650 us (95%)
  matrix products  31.5 us (2%)
  local copies, waits for them, and re-layouts  28.1 us (2%)
    psum x8, waiting for transfers between devices, advance(): panel_solved = lax.psum(term, 'row')  1490 us
    all_gather x1, waiting for transfers between devices, shards(): whole_factor = lax.all_gather(factor, 'col', axis=1, tiled=True)  161 us
  transfers between devices with their start and end apart: 9, of which 9 were waited for; matrix products, arithmetic and copies ran while one was open for 0% of the time, Pallas kernels for 0%

commit v1 on v0

--- a/solution.py
+++ b/solution.py
@@ -13,7 +13,9 @@
     my_offset = my_row % per_panel * rows_here
     local_blocks = factor.shape[1]
     panel_count = local_blocks * lax.axis_size("col") // per_panel
-    whole_factor = lax.all_gather(factor, "col", axis=1, tiled=True)
+    whole_factor = jnp.concatenate(
+        lax.all_to_all(jnp.stack([factor] * lax.axis_size("col")), "col", 0, 0), axis=1
+    )
     flat_factor = whole_factor.reshape(rows_here, -1)
     empty = jnp.zeros(phenotypes.shape, jnp.float32)
 

time: 1740 us -> 1790 us (1.029)
  waiting for transfers between devices: 1650 us -> 1670 us
    all_to_all x0 -> x1, waiting for transfers between devices: none -> 181 us  [shards(): lax.all_to_all(jnp.stack([factor] * lax.axis_size('col')), 'col', 0, 0)]
    all_gather x1 -> x0, waiting for transfers between devices: 161 us -> none  [shards(): whole_factor = lax.all_gather(factor, 'col', axis=1, tiled=True)]
    all_to_all x0 -> x1, local copies, waits for them, and re-layouts: none -> 19.2 us  [shards(): lax.all_to_all(jnp.stack([factor] * lax.axis_size('col')), 'col', 0, 0)]
    unnamed x3 -> x2, local copies, waits for them, and re-layouts: 18.6 us -> 0.01 us
where the time goes in v1:
time: 1790 us
  waiting for transfers between devices  1670 us (93%)
  matrix products  44.5 us (2%)
  local copies, waits for them, and re-layouts  39.3 us (2%)
    psum x8, waiting for transfers between devices, advance(): panel_solved = lax.psum(term, 'row')  1490 us
    all_to_all x1, waiting for transfers between devices, shards(): lax.all_to_all(jnp.stack([factor] * lax.axis_size('col')), 'col', 0, 0)  181 us
    dot_general x8, matrix products, advance(): jnp.dot(columns, panel_solved, precision=lax.Precision.HIGHEST, preferred...  42.4 us
  transfers between devices with their start and end apart: 9, of which 9 were waited for; matrix products, arithmetic and copies ran while one was open for 0% of the time, Pallas kernels for 0%

profile of v1, /device:TPU:2, one launch (start us, length us, event | category | flops | bytes accessed | tf_op | source)
XLA Modules:
  0.0 1788.3 jit_solution(10567511947867886816)
XLA Ops:
  6.5 10.5 stack.2
  17.0 9.2 all-to-all-start
  26.2 180.6 %all-to-all-done = f32[4,256,16,256]{3,2,1,0:T(8,128)} async-done(((f32[4,256,16,256]{3,2,1,0:T(8,128)}), f32[4,256,16,256]{3,2,1,0:T(8,128)}, u32[]{:S(2)}, u32[]{:S(2)}) %all-to-all-start) | async-done | bytes 16777248 | tf_op jit(solution)/shard_map/all_to_all | solution.py:17
  206.8 19.2 %copy.6 = f32[4,256,16,256]{1,3,2,0:T(8,128)} copy(f32[4,256,16,256]{3,2,1,0:T(8,128)} %all-to-all-done) | data formatting | bytes 33554432 | tf_op jit(solution)/shard_map/all_to_all | solution.py:17
  226.1 1554.6 %while.18 = (s32[]{:T(128)}, f32[256,128]{1,0:T(8,128)S(1)}, f32[256,128]{0,1:T(8,128)S(1)}, f32[256,16384]{0,1:T(8,128)}, s32[]{:T(128)}, /*index=5*/f32[256,12...) while((s32[]{:T(128)}, f32[256,128]{1,0:T(8,128)S(1)}, ...), condition=%wide.region_4.5_spmd.clone, body=%wide.region_0.4_spmd.clone.sunk | while | flops 1611038720 | bytes 17957160 | solution.py:50
  226.1 2.2 conditional.3
  226.1 2.1 convolution_bitcast_fusion
  228.3 1.0 copy-done
  229.3 188.4 %all-reduce.2.cloned.1.call-done = f32[2048,128]{0,1:T(8,128)} async-done(((f32[2048,128]{0,1:T(8,128)}), f32[2048,128]{0,1:T(8,128)}) %all-reduce.2.cloned.1.call-update) | async-done | bytes 1048592 | tf_op jit(solution)/shard_map/while/body/eval_jaxpr/psum | solution.py:39
  417.7 5.3 fusion.14
  423.0 0.9 select_select_fusion.2
  424.1 0.1 conditional.3
  424.2 1.0 copy-done
  425.2 186.5 %all-reduce.2.cloned.1.call-done = f32[2048,128]{0,1:T(8,128)} async-done(((f32[2048,128]{0,1:T(8,128)}), f32[2048,128]{0,1:T(8,128)}) %all-reduce.2.cloned.1.call-update) | async-done | bytes 1048592 | tf_op jit(solution)/shard_map/while/body/eval_jaxpr/psum | solution.py:39
  611.7 5.3 fusion.14
  617.0 0.9 select_select_fusion.2
  618.0 0.1 conditional.3
  618.2 1.0 copy-done
  619.2 186.5 %all-reduce.2.cloned.1.call-done = f32[2048,128]{0,1:T(8,128)} async-done(((f32[2048,128]{0,1:T(8,128)}), f32[2048,128]{0,1:T(8,128)}) %all-reduce.2.cloned.1.call-update) | async-done | bytes 1048592 | tf_op jit(solution)/shard_map/while/body/eval_jaxpr/psum | solution.py:39
  805.7 5.3 fusion.14
  811.0 0.9 select_select_fusion.2
  812.1 0.1 conditional.3
  812.2 1.0 copy-done
  813.2 186.1 %all-reduce.2.cloned.1.call-done = f32[2048,128]{0,1:T(8,128)} async-done(((f32[2048,128]{0,1:T(8,128)}), f32[2048,128]{0,1:T(8,128)}) %all-reduce.2.cloned.1.call-update) | async-done | bytes 1048592 | tf_op jit(solution)/shard_map/while/body/eval_jaxpr/psum | solution.py:39
  999.4 5.3 fusion.14
  1004.7 0.9 select_select_fusion.2
  1005.7 0.1 conditional.3
  1005.7 0.1 broadcast.6
  1005.9 1.0 copy-done
  1006.9 186.2 %all-reduce.2.cloned.1.call-done = f32[2048,128]{0,1:T(8,128)} async-done(((f32[2048,128]{0,1:T(8,128)}), f32[2048,128]{0,1:T(8,128)}) %all-reduce.2.cloned.1.call-update) | async-done | bytes 1048592 | tf_op jit(solution)/shard_map/while/body/eval_jaxpr/psum | solution.py:39
  1193.1 5.3 fusion.14
  1198.4 0.9 select_select_fusion.2
  1199.4 0.1 conditional.3
  1199.6 1.0 copy-done
  1200.6 185.9 %all-reduce.2.cloned.1.call-done = f32[2048,128]{0,1:T(8,128)} async-done(((f32[2048,128]{0,1:T(8,128)}), f32[2048,128]{0,1:T(8,128)}) %all-reduce.2.cloned.1.call-update) | async-done | bytes 1048592 | tf_op jit(solution)/shard_map/while/body/eval_jaxpr/psum | solution.py:39
  1386.5 5.3 fusion.14
  1391.8 0.9 select_select_fusion.2
  1392.8 0.1 conditional.3
  1392.9 1.0 copy-done
  1394.0 186.5 %all-reduce.2.cloned.1.call-done = f32[2048,128]{0,1:T(8,128)} async-done(((f32[2048,128]{0,1:T(8,128)}), f32[2048,128]{0,1:T(8,128)}) %all-reduce.2.cloned.1.call-update) | async-done | bytes 1048592 | tf_op jit(solution)/shard_map/while/body/eval_jaxpr/psum | solution.py:39
  1580.4 5.3 fusion.14
  1585.7 0.9 select_select_fusion.2
  1586.8 0.1 conditional.3
  1586.9 1.0 copy-done
  1588.0 186.5 %all-reduce.2.cloned.1.call-done = f32[2048,128]{0,1:T(8,128)} async-done(((f32[2048,128]{0,1:T(8,128)}), f32[2048,128]{0,1:T(8,128)}) %all-reduce.2.cloned.1.call-update) | async-done | bytes 1048592 | tf_op jit(solution)/shard_map/while/body/eval_jaxpr/psum | solution.py:39
  1774.5 5.3 fusion.14
  1779.8 0.9 select_select_fusion.2
  1780.7 0.8 copy.8
  (42 shorter events, 1.1 us)
Async XLA Ops:
  17.0 189.8 %all-to-all-start = ((f32[4,256,16,256]{3,2,1,0:T(8,128)}), f32[4,256,16,256]{3,2,1,0:T(8,128)}, u32[]{:S(2)}, u32[]{:S(2)}) async-start(f32[4,256,16,256]{3,2,1,0:T(8,128)} %stack.2), calls=%async_computation | async-start | bytes 33554432 | tf_op jit(solution)/shard_map/all_to_all | solution.py:17
  26.2 199.9 %copy-start.1 = (f32[256,2048]{1,0:T(8,128)S(1)}, f32[256,2048]{1,0:T(8,128)}, u32[]{:S(2)}) copy-start(f32[256,2048]{1,0:T(8,128)} %param.8) | copy-start | bytes 6291460
  226.1 191.7 %all-reduce.2.cloned.1.call-start = ((), (), s32[]{:S(2)}) async-start(), calls=%async_computation.1 | async-start | bytes 2097152 | tf_op jit(solution)/shard_map/while/body/eval_jaxpr/psum | solution.py:39
  228.3 1.0 copy-start
  424.0 187.7 %all-reduce.2.cloned.1.call-start = ((), (), s32[]{:S(2)}) async-start(), calls=%async_computation.1 | async-start | bytes 2097152 | tf_op jit(solution)/shard_map/while/body/eval_jaxpr/psum | solution.py:39
  424.2 1.0 copy-start
  618.0 187.7 %all-reduce.2.cloned.1.call-start = ((), (), s32[]{:S(2)}) async-start(), calls=%async_computation.1 | async-start | bytes 2097152 | tf_op jit(solution)/shard_map/while/body/eval_jaxpr/psum | solution.py:39
  618.2 1.0 copy-start
  812.0 187.4 %all-reduce.2.cloned.1.call-start = ((), (), s32[]{:S(2)}) async-start(), calls=%async_computation.1 | async-start | bytes 2097152 | tf_op jit(solution)/shard_map/while/body/eval_jaxpr/psum | solution.py:39
  812.2 1.0 copy-start
  1005.6 187.4 %all-reduce.2.cloned.1.call-start = ((), (), s32[]{:S(2)}) async-start(), calls=%async_computation.1 | async-start | bytes 2097152 | tf_op jit(solution)/shard_map/while/body/eval_jaxpr/psum | solution.py:39
  1005.8 1.0 copy-start
  1199.3 187.1 %all-reduce.2.cloned.1.call-start = ((), (), s32[]{:S(2)}) async-start(), calls=%async_computation.1 | async-start | bytes 2097152 | tf_op jit(solution)/shard_map/while/body/eval_jaxpr/psum | solution.py:39
  1199.5 1.0 copy-start
  1392.7 187.7 %all-reduce.2.cloned.1.call-start = ((), (), s32[]{:S(2)}) async-start(), calls=%async_computation.1 | async-start | bytes 2097152 | tf_op jit(solution)/shard_map/while/body/eval_jaxpr/psum | solution.py:39
  1392.9 1.0 copy-start
  1586.7 187.7 %all-reduce.2.cloned.1.call-start = ((), (), s32[]{:S(2)}) async-start(), calls=%async_computation.1 | async-start | bytes 2097152 | tf_op jit(solution)/shard_map/while/body/eval_jaxpr/psum | solution.py:39
  1586.9 1.0 copy-start
Sparse Core Ops, SparseCore 0:
  230.3 187.3 all-reduce.1
  428.2 183.4 all-reduce.1
  622.2 183.4 all-reduce.1
  815.9 183.4 all-reduce.1
  1009.6 183.4 all-reduce.1
  1203.3 183.1 all-reduce.1
  1397.0 183.4 all-reduce.1
  1591.0 183.4 all-reduce.1
